TPU v7x, 32 devices: a whole 2x2x4 slice. The times are simulated.
32 devices in a mesh: groups: 2 (over y), dp: 4 (over x, core), ctx: 4 (over z).
Axes of the slice: x: 2, y: 2, z: 4, core: 2. Of those that a mesh axis runs over, the one named last changes fastest.
Arguments:
- normed_input: bfloat16 [8, 1024, 4096], P(('groups', 'dp'), 'ctx'), parts along dimension 0, may hold values from -6 to 6
- query_weight: bfloat16 [4096, 1024], P(('dp', 'ctx')), may hold values from -0.09375 to 0.09375
- key_vectors: bfloat16 [8, 1024, 1024], P(('groups', 'dp'), 'ctx'), parts along dimension 0, may hold values from -6 to 6
- value_vectors: bfloat16 [8, 1024, 1024], P(('groups', 'dp'), 'ctx'), parts along dimension 0, may hold values from -6 to 6
- input_gate: float32 [8, 4, 1024], P(('groups', 'dp'), None, 'ctx'), parts along dimension 0, may hold values from -16 to 210
- forget_gate: float32 [8, 4, 1024], P(('groups', 'dp'), None, 'ctx'), parts along dimension 0
- resets: int32 [8, 1024], P(('groups', 'dp'), 'ctx'), parts along dimension 0, may hold values 0 or 1
Outputs:
- hidden: bfloat16 [8, 1024, 1024], P(('groups', 'dp'), 'ctx'), parts along dimension 0
There are 2 independent parts, one for each index of `groups`. A program takes and returns all parts, laid end to end along the dimension named above; an argument that names none is the same for every part. Nothing has to cross between parts.
Inputs may be any that keep to these rules, and one draw needn't show every extreme that they name: `resets`: 1 where a new document begins at that position.
All inputs are finite; a program needn't handle non-finite values. No bound on the sum of `resets` on one device may be relied on, other than what follows from the above.
Results may differ from a plain program's by a relative error of at most 0.009.
Values may be sent and summed in bfloat16 or wider, within the bound.
A program may use at most 128 MiB of HBM per device.

v0:
```python
import jax
import jax.numpy as jnp
from jax import lax
from jax.sharding import PartitionSpec as P

very_low = -1e30


def prefix(part, axis, combine, identity):
    place = lax.axis_index(axis)
    gathered = jax.tree.map(lambda a: lax.all_gather(a, axis), part)
    state = jax.tree.map(lambda a, e: jnp.zeros_like(a) + jnp.asarray(e, a.dtype), part, identity)

    def one(hop, state):
        return combine(
            state, jax.tree.map(lambda a: lax.dynamic_index_in_dim(a, hop, 0, False), gathered)
        )

    return lax.fori_loop(0, place, one, state)


def combine(earlier, later):
    gap_early, memory_early, normer_early, top_early = earlier
    gap_late, memory_late, normer_late, top_late = later
    shifted = top_early + gap_late
    top_both = jnp.maximum(shifted, top_late)
    early_weight = jnp.exp(shifted - top_both)
    late_weight = jnp.exp(top_late - top_both)
    matrix_memory = (
        early_weight[..., None, None] * memory_early + late_weight[..., None, None] * memory_late
    )
    normer = early_weight[..., None] * normer_early + late_weight[..., None] * normer_late
    gap_total = jnp.maximum(gap_early + gap_late, very_low)
    return (gap_total, matrix_memory, normer, top_both)


def make_adder(source, piece):
    return jnp.dot(source, piece, preferred_element_type=jnp.float32)


def body(normed_input, query_weight, key_vectors, value_vectors, input_gate, forget_gate, resets):
    sequences, length, features = normed_input.shape
    head_count = input_gate.shape[1]
    key_size = key_vectors.shape[2] // head_count
    value_size = value_vectors.shape[2] // head_count
    score_factor = key_size ** (-0.5)
    flat_rows = normed_input.reshape(sequences * length, features)
    key_heads = key_vectors.reshape(sequences, length, head_count, key_size)
    value_heads = value_vectors.reshape(sequences, length, head_count, value_size)
    log_forget = jax.nn.log_sigmoid(forget_gate)
    reset_count = jnp.cumsum(resets, axis=1)
    cumulative = jnp.cumsum(log_forget, axis=2)
    chain_total = cumulative[:, :, -1]
    final_count = reset_count[:, -1:]
    alive_end = reset_count == final_count
    end_expo = jnp.where(
        alive_end[:, None, :], chain_total[:, :, None] - cumulative + input_gate, very_low
    )
    own_max = jnp.max(end_expo, axis=2)
    token_weight = jnp.exp(end_expo - own_max[:, :, None])
    key_weighted = (
        key_heads.astype(jnp.float32) * jnp.transpose(token_weight, (0, 2, 1))[..., None]
    ).astype(jnp.bfloat16)
    own_memory = jnp.einsum(
        "slhk,slhv->shkv", key_weighted, value_heads, preferred_element_type=jnp.float32
    )
    own_normer = jnp.sum(key_weighted.astype(jnp.float32), axis=1)
    gap_own = jnp.where(final_count > 0, very_low, chain_total)
    identity = (
        jnp.zeros_like(gap_own),
        jnp.zeros_like(own_memory),
        jnp.zeros_like(own_normer),
        jnp.full_like(own_max, very_low),
    )
    carried_state = prefix((gap_own, own_memory, own_normer, own_max), "ctx", combine, identity)
    memory_before = carried_state[1].astype(jnp.bfloat16)
    normer_before = carried_state[2].astype(jnp.bfloat16)
    max_before = carried_state[3]
    query_sum = make_adder(
        flat_rows, lax.all_gather(query_weight, ("dp", "ctx"), axis=0, tiled=True)
    )
    projected = query_sum.astype(jnp.bfloat16).reshape(sequences, length, head_count, key_size)
    scores = (
        jnp.einsum("slhk,sthk->shlt", projected, key_heads, preferred_element_type=jnp.float32)
        * score_factor
    )
    positions = jnp.arange(length)
    causal = positions[:, None] >= positions[None, :]
    same_doc = reset_count[:, :, None] == reset_count[:, None, :]
    linked = jnp.logical_and(same_doc, causal[None])
    exponent = jnp.where(
        linked[:, None],
        cumulative[:, :, :, None] - cumulative[:, :, None, :] + input_gate[:, :, None, :],
        very_low,
    )
    carried = jnp.where(reset_count[:, None, :] == 0, cumulative + max_before[:, :, None], very_low)
    cross_numerator = (
        jnp.einsum("slhk,shkv->slhv", projected, memory_before, preferred_element_type=jnp.float32)
        * score_factor
    )
    inter_den = (
        jnp.einsum("slhk,shk->slh", projected, normer_before, preferred_element_type=jnp.float32)
        * score_factor
    )
    row_max = jnp.maximum(jnp.max(exponent, axis=3), carried)
    weighted_scores = (jnp.exp(exponent - row_max[..., None]) * scores).astype(jnp.bfloat16)
    carry_scale = jnp.transpose(jnp.exp(carried - row_max), (0, 2, 1))
    numerator = (
        jnp.einsum(
            "shlt,sthv->slhv", weighted_scores, value_heads, preferred_element_type=jnp.float32
        )
        + carry_scale[..., None] * cross_numerator
    )
    denominator = (
        jnp.transpose(jnp.sum(weighted_scores.astype(jnp.float32), axis=3), (0, 2, 1))
        + carry_scale * inter_den
    )
    floor_value = jnp.transpose(jnp.exp(jnp.maximum(-row_max, 0.0)), (0, 2, 1))
    hidden = numerator / jnp.maximum(jnp.abs(denominator), floor_value)[..., None]
    return hidden.reshape(sequences, length, head_count * value_size).astype(jnp.bfloat16)


def solution(mesh):
    return jax.shard_map(
        body,
        mesh=mesh,
        in_specs=(
            P(("groups", "dp"), "ctx", None),
            P(("dp", "ctx"), None),
            P(("groups", "dp"), "ctx", None),
            P(("groups", "dp"), "ctx", None),
            P(("groups", "dp"), None, "ctx"),
            P(("groups", "dp"), None, "ctx"),
            P(("groups", "dp"), "ctx"),
        ),
        out_specs=P(("groups", "dp"), "ctx", None),
        check_vma=False,
    )
```

profile of v0, /device:TPU:0, one launch (start us, length us, event | category | flops | bytes accessed | tf_op | source)
XLA Modules:
  0.0 203.0 jit_solution(4821478915440849661)
XLA Ops:
  6.5 0.9 fusion.22
  7.4 1.2 reduce-window.16
  8.7 1.0 reduce-window.14
  9.7 0.2 slice_reduce_fusion.1
  9.9 0.6 slice.25
  10.5 0.2 reduce-window.15
  10.8 0.7 slice.26
  13.2 0.2 slice_reduce_fusion
  13.4 0.9 fusion.29
  14.2 0.8 exponential_bitcast_fusion.2
  15.0 1.2 copy.114
  16.3 2.2 %copy.115 = bf16[1,256,1024]{1,2,0:T(8,128)(2,1)} copy(bf16[1,256,1024]{2,1,0:T(8,128)(2,1)} %param.11) | data formatting | bytes 1048576 | tf_op jit(solution)/shard_map/reshape | solution.py:48
  18.5 2.4 %fusion.17 = f32[4,256,256]{2,1,0:T(8,128)} fusion(bf16[256,4,256]{0,2,1:T(8,128)(2,1)S(1)} %bitcast.156, bf16[256,4,256]{0,2,1:T(8,128)(2,1)} %bitcast.162, f32[256,4]{0,1:T(4,128)S(1)} %exponential_bitcast_fusion.2), kind=kOutput, calls=%fused_computation.29 | convolution fusion | flops 135004160 | bytes 2101248 | tf_op jit(solution)/shard_map/slhk,slhv->shkv/dot_general | solution.py:64
  21.0 0.7 all-gather.6.cloned.1.call-update
  21.8 12.5 %all-gather = f32[4,4,1]{1,2,0:T(1,128)S(1)} all-gather(f32[1,4,1]{1,2,0:T(1,128)S(1)} %copy.94), channel_id=2, replica_groups=mesh['groups'=2,'dp'=4,'ctx'=4] {'ctx'}, dimensions={0}, use_global_device_ids=true | all-gather | bytes 80 | tf_op jit(solution)/shard_map/all_gather | solution.py:11
  34.4 0.6 dynamic-slice
  35.5 0.2 dynamic-update-slice
  35.8 8.9 %all-reduce = f32[16]{0:T(128)S(1)} all-reduce(f32[16]{0:T(128)S(1)} %dynamic-update-slice), channel_id=3, replica_groups=mesh['groups'=2,'dp'=4,'ctx'=4] {'ctx'}, use_global_device_ids=true, to_apply=%add | all-reduce | flops 16 | bytes 128
  45.1 1.1 mul.131
  46.1 2.5 %copy.113 = f32[1,256,1024]{2,1,0:T(8,128)} copy(f32[1,256,1024]{1,2,0:T(8,128)} %bitcast.158) | data formatting | bytes 2097152 | tf_op jit(solution)/shard_map/mul | solution.py:62
  48.7 1.4 convert_reduce_fusion.1
  50.1 13.6 %all_gather.31 = f32[4,1,4,256]{3,2,1,0:T(4,128)S(1)} all-gather(f32[1,1,4,256]{3,2,1,0:T(4,128)S(1)} %all_gather.30), channel_id=1, replica_groups=mesh['groups'=2,'dp'=4,'ctx'=4] {'ctx'}, dimensions={0}, use_global_device_ids=true | all-gather | bytes 20480 | tf_op jit(solution)/shard_map/all_gather | solution.py:11
  63.7 0.4 select_reduce_fusion
  64.1 40.8 %all-gather.8.cloned.1.call-done = f32[16,256,256]{2,1,0:T(8,128)} async-done(((f32[4,256,256]{2,1,0:T(8,128)}), f32[16,256,256]{2,1,0:T(8,128)}) %all-gather.8.cloned.1.call-update) | async-done | bytes 4194320 | tf_op jit(solution)/shard_map/all_gather | solution.py:11
  105.1 75.6 %all-gather.6.cloned.1.call-done = bf16[4096,1024]{1,0:T(8,128)(2,1)} async-done(((bf16[256,1024]{1,0:T(8,128)(2,1)}), bf16[4096,1024]{1,0:T(8,128)(2,1)}) %all-gather.6.cloned.1.call-update) | async-done | bytes 8388624 | tf_op jit(solution)/shard_map/all_gather | solution.py:80
  180.7 6.6 %fusion.13 = bf16[256,1024]{1,0:T(8,128)(2,1)} fusion(bf16[4096,1024]{1,0:T(8,128)(2,1)} %all-gather.6.cloned.1.call-done, bf16[1,256,4096]{2,1,0:T(8,128)(2,1)S(1)} %copy-done), kind=kOutput, calls=%fused_computation.22 | convolution fusion | flops 2147745792 | bytes 11010048 | tf_op jit(solution)/shard_map/dot_general | solution.py:38
  187.3 2.1 %copy.116 = bf16[256,1024]{0,1:T(8,128)(2,1)} copy(bf16[256,1024]{1,0:T(8,128)(2,1)} %fusion.13) | data formatting | bytes 1048576 | tf_op jit(solution)/shard_map/reshape.36
  189.4 1.3 fusion.27
  190.7 1.8 convert_reduce_fusion
  192.6 0.3 convolution_bitcast_fusion
  193.0 1.2 fusion.16
  194.1 2.0 %copy.107 = bf16[1,256,1024]{2,1,0:T(8,128)(2,1)} copy(bf16[1,256,1024]{1,2,0:T(8,128)(2,1)} %bitcast.164) | data formatting | bytes 1048576 | tf_op jit(solution)/shard_map/convert_element_type | solution.py:120
  (46 shorter events, 1.5 us)
Async XLA Ops:
  6.5 174.2 %copy-start = (bf16[1,256,4096]{2,1,0:T(8,128)(2,1)S(1)}, bf16[1,256,4096]{2,1,0:T(8,128)(2,1)}, u32[]{:S(2)}) copy-start(bf16[1,256,4096]{2,1,0:T(8,128)(2,1)} %param.9) | copy-start | bytes 6291460
  6.5 27.8 %copy-start.6 = (u32[32]{0:T(128)S(1)}, u32[32]{0:T(128)}, u32[]{:S(2)}) copy-start(u32[32]{0:T(128)} %constant.62) | copy-start | bytes 388
  6.5 98.4 %all-gather.8.cloned.1.call-start = ((), (), s32[]{:S(2)}) async-start(), calls=%async_computation.1 | async-start | bytes 5242880 | tf_op jit(solution)/shard_map/all_gather | solution.py:11
  16.3 33.8 %copy-start.1 = (bf16[1,256,1024]{1,2,0:T(8,128)(2,1)}, bf16[1,256,1024]{1,2,0:T(8,128)(2,1)S(1)}, u32[]{:S(2)}) copy-start(bf16[1,256,1024]{1,2,0:T(8,128)(2,1)S(1)} %copy.114) | copy-start | bytes 1572868
  16.3 32.4 %copy-start.3 = (bf16[1,256,1024]{2,1,0:T(8,128)(2,1)S(1)}, bf16[1,256,1024]{2,1,0:T(8,128)(2,1)}, u32[]{:S(2)}) copy-start(bf16[1,256,1024]{2,1,0:T(8,128)(2,1)} %param.11) | copy-start | bytes 1572868
  18.5 45.2 %copy-start.5 = (f32[1,4,256]{2,1,0:T(4,128)S(1)}, f32[1,4,256]{2,1,0:T(4,128)}, u32[]{:S(2)}) copy-start(f32[1,4,256]{2,1,0:T(4,128)} %param.13) | copy-start | bytes 12292
  21.0 159.8 %all-gather.6.cloned.1.call-start = ((), (), s32[]{:S(2)}) async-start(), calls=%async_computation | async-start | bytes 8912896 | tf_op jit(solution)/shard_map/all_gather | solution.py:80
  189.4 3.1 %copy-start.2 = (bf16[1,256,1024]{1,2,0:T(8,128)(2,1)S(1)}, bf16[1,256,1024]{1,2,0:T(8,128)(2,1)}, u32[]{:S(2)}) copy-start(bf16[1,256,1024]{1,2,0:T(8,128)(2,1)} %copy-done.1) | copy-start | bytes 1572868
  189.4 3.5 %copy-start.4 = (bf16[256,1024]{0,1:T(8,128)(2,1)S(1)}, bf16[256,1024]{0,1:T(8,128)(2,1)}, u32[]{:S(2)}) copy-start(bf16[256,1024]{0,1:T(8,128)(2,1)} %copy.116) | copy-start | bytes 1572868
Sparse Core Ops, SparseCore 0:
  21.1 83.8 all-gather.7
  107.2 73.5 all-gather.5
where the time goes:
time: 204 us; the launch traced here: 203 us
  waiting for transfers between devices  117 us (57%)
  blocking collectives  35 us (17%)
  between operations  15.5 us (8%)
  local copies, waits for them, and re-layouts  14.5 us (7%)
  matrix products  13.6 us (7%)
  other arithmetic  7.22 us (4%)
    all_gather x1, waiting for transfers between devices, body(): lax.all_gather(query_weight, ('dp', 'ctx'), axis=0, tiled=True)  75.6 us
    all_gather x1, waiting for transfers between devices, prefix(): gathered = jax.tree.map(lambda a: lax.all_gather(a, axis), part)  40.8 us
    all_gather x2, blocking collectives, prefix(): gathered = jax.tree.map(lambda a: lax.all_gather(a, axis), part)  26.1 us
    unnamed x1, blocking collectives  8.92 us
    dot_general x1, matrix products, make_adder(): return jnp.dot(source, piece, preferred_element_type=jnp.float32)  6.55 us
  transfers between devices with their start and end apart: 2, of which 2 were waited for; matrix products, arithmetic and copies ran while one was open for 3% of the time, Pallas kernels for 0%

commit v1 on v0

v1 whole, which is shorter than its diff:
```python
import functools

import jax
import jax.numpy as jnp
from jax import lax
from jax.experimental import pallas as pl
from jax.experimental.pallas import tpu as pltpu
from jax.sharding import PartitionSpec as P

very_low = -1e30
shared_columns = 384
MESH = pl.DeviceIdType.MESH


def dot(a, b, dims=((1,), (0,))):
    return lax.dot_general(a, b, (dims, ((), ())), preferred_element_type=jnp.float32)


def kernel(
    spread, Z, heads, x_hbm, w_hbm, k_hbm, v_hbm, ig_ref, fg_ref, rs_ref, out_ref,
    xv, kv, vv, wown, wbuf, acc, prob, stack, imax_scr, own_mem, own_info,
    mem_in, info_in, mem_out, info_out,
    lsem, zsend, zrecv, xsend, xrecv, ysend, yrecv, csend, crecv, ssend, srecv,
):
    y = lax.axis_index("groups")
    d = lax.axis_index("dp")
    z = lax.axis_index("ctx")
    x, c = d // 2, d % 2
    up, down = (y, d, z + 1), (y, d, z - 1)
    across = (y, (1 - x) * 2 + c, z)
    over = (1 - y, d, z)
    mate = (y, x * 2 + 1 - c, z)
    length, features = xv.shape
    dk = kv.shape[1] // heads
    dv = vv.shape[1] // heads
    factor = dk ** (-0.5)
    width = acc.shape[1]
    rows = wbuf.shape[1]
    A = shared_columns

    local = [
        pltpu.make_async_copy(k_hbm.at[0], kv, lsem.at[0]),
        pltpu.make_async_copy(v_hbm.at[0], vv, lsem.at[1]),
        pltpu.make_async_copy(x_hbm.at[0], xv, lsem.at[2]),
        pltpu.make_async_copy(w_hbm, wown, lsem.at[3]),
    ]
    for one in local:
        one.start()

    barrier = pltpu.get_barrier_semaphore()

    def greet(device):
        pl.semaphore_signal(barrier, inc=1, device_id=device, device_id_type=MESH)

    @pl.when(z < Z - 1)
    def _():
        greet(up)

    @pl.when(z > 0)
    def _():
        greet(down)

    base = 0
    if spread:
        for device in (across, over, mate):
            greet(device)
        base = 3
    pl.semaphore_wait(
        barrier, base + jnp.where(z > 0, 1, 0) + jnp.where(z < Z - 1, 1, 0)
    )

    def columns(part):
        if part == 0:
            return pl.ds(pl.multiple_of(y * A, 128), A)
        if part == 1:
            return pl.ds(pl.multiple_of((1 - y) * A, 128), A)
        return pl.ds(2 * A, width - 2 * A)

    def shard(xx, cc, zz):
        return (xx * 2 + cc) * Z + zz

    def remote(xx, cc, zz, part, send, recv, device, own=False):
        there = wbuf.at[shard(xx, cc, zz), :, columns(part)]
        here = w_hbm.at[:, columns(part)] if own else there
        return pltpu.make_async_remote_copy(
            src_ref=here, dst_ref=there, send_sem=send, recv_sem=recv,
            device_id=device, device_id_type=MESH,
        )

    def z_copy(way, zz, part, own=False):
        device = up if way == 0 else down
        return remote(x, c, zz, part, zsend.at[way, zz, part // 2], zrecv.at[zz, part // 2], device, own)

    def x_copy(xx, zz, part, own=False):
        return remote(xx, c, zz, part, xsend.at[zz, part // 2], xrecv.at[zz, part // 2], across, own)

    def y_copy(xx, zz, part):
        return remote(xx, c, zz, part, ysend.at[xx, zz], yrecv.at[xx, zz], over)

    def c_copy(xx, cc, zz, part, own=False):
        return remote(xx, cc, zz, part, csend.at[xx, zz, part], crecv.at[xx, zz, part], mate, own)

    if spread:
        for part in (0, 2):
            @pl.when(z < Z - 1)
            def _():
                z_copy(0, z, part, True).start()

            @pl.when(z > 0)
            def _():
                z_copy(1, z, part, True).start()

            x_copy(x, z, part, True).start()
        for part in (0, 1, 2):
            c_copy(x, c, z, part, True).start()

    g = ig_ref[0]
    f = fg_ref[0]
    stack[...] = jnp.zeros_like(stack)
    stack[0:heads, :] = jnp.minimum(f, 0.0) - jnp.log1p(jnp.exp(-jnp.abs(f)))
    stack[4:5, :] = rs_ref[...].astype(jnp.float32)
    run = stack[0:8, :]
    lane = lax.broadcasted_iota(jnp.int32, run.shape, 1)
    hop = 1
    while hop < length:
        run = run + jnp.where(lane >= hop, pltpu.roll(run, hop, 1), 0.0)
        hop *= 2
    stack[0:8, :] = run
    stack[8:8 + heads, :] = g
    cols = stack[...].T
    count_row, count_col = run[4:5, :], cols[:, 4:5]
    count_last = run[4:5, length - 1:length]

    def cum_col(h):
        return cols[:, h:h + 1]

    def cum_last(h):
        return run[h:h + 1, length - 1:length]

    for one in local[:2]:
        one.wait()

    for h in range(heads):
        end_row = jnp.where(count_row == count_last, cum_last(h) - run[h:h + 1, :] + g[h:h + 1, :], very_low)
        top = jnp.max(end_row, axis=1, keepdims=True)
        end_col = jnp.where(
            count_col == count_last, cum_last(h) - cum_col(h) + cols[:, 8 + h:9 + h], very_low
        )
        weighted = (
            kv[:, h * dk:(h + 1) * dk].astype(jnp.float32) * jnp.exp(end_col - top)
        ).astype(jnp.bfloat16)
        own_mem[h] = dot(weighted, vv[:, h * dv:(h + 1) * dv], ((0,), (0,)))
        own_info[h:h + 1, :] = jnp.sum(weighted.astype(jnp.float32), axis=0, keepdims=True)
        own_info[heads + h:heads + h + 1, :] = jnp.broadcast_to(top, (1, dk))

    def info_copy():
        return pltpu.make_async_remote_copy(
            src_ref=info_out, dst_ref=info_in, send_sem=ssend.at[heads], recv_sem=srecv.at[heads],
            device_id=up, device_id_type=MESH,
        )

    def mem_copy(h):
        return pltpu.make_async_remote_copy(
            src_ref=mem_out.at[h], dst_ref=mem_in.at[h], send_sem=ssend.at[h], recv_sem=srecv.at[h],
            device_id=up, device_id_type=MESH,
        )

    def pass_state():
        @pl.when(z > 0)
        def _():
            info_copy().wait_recv()

        @pl.when(z == 0)
        def _():
            mem_in[...] = jnp.zeros_like(mem_in)
            info_in[0:heads, :] = jnp.zeros((heads, dk), jnp.float32)
            info_in[heads:, :] = jnp.full((heads, dk), very_low, jnp.float32)

        @pl.when(z < Z - 1)
        def _():
            info = info_in[...]
            own = own_info[...]
            early, late = [], []
            for h in range(heads):
                gap = jnp.where(count_last > 0, very_low, cum_last(h))
                shifted = info[heads + h:heads + h + 1, :] + gap
                top = own[heads + h:heads + h + 1, :]
                both = jnp.maximum(shifted, top)
                early.append(jnp.exp(shifted - both))
                late.append(jnp.exp(top - both))
                info_out[h:h + 1, :] = early[h] * info[h:h + 1, :] + late[h] * own[h:h + 1, :]
                info_out[heads + h:heads + h + 1, :] = both
            info_copy().start()
            for h in range(heads):
                @pl.when(z > 0)
                def _():
                    mem_copy(h).wait_recv()

                mem_out[h] = (
                    early[h][:, 0:1] * mem_in[h].astype(jnp.float32) + late[h][:, 0:1] * own_mem[h]
                ).astype(jnp.bfloat16)
                mem_copy(h).start()

        @pl.when(z == Z - 1)
        def _():
            @pl.when(z > 0)
            def _():
                for h in range(heads):
                    mem_copy(h).wait_recv()

    if spread:
        @pl.when(z == 0)
        def _():
            pass_state()
    else:
        pass_state()

    row_at = lax.broadcasted_iota(jnp.int32, (length, length), 0)
    col_at = lax.broadcasted_iota(jnp.int32, (length, length), 1)
    linked = jnp.logical_and(count_col == count_row, row_at >= col_at)
    for h in range(heads):
        exponent = jnp.where(linked, cum_col(h) - run[h:h + 1, :] + g[h:h + 1, :], very_low)
        top = jnp.max(exponent, axis=1, keepdims=True)
        imax_scr[:, h:h + 1] = top
        prob[h] = jnp.exp(exponent - top) * factor

    for one in local[2:]:
        one.wait()

    def multiply(at, piece):
        part = xv[:, pl.ds(pl.multiple_of(at * rows, 128), rows)]
        acc[...] += dot(part, piece)

    if spread:
        acc[...] = dot(xv[:, pl.ds(pl.multiple_of(shard(x, c, z) * rows, 128), rows)], wown[...])

        def places(q, low):
            below, above = z - q, z + q
            yield below, jnp.logical_and(q >= low, jnp.logical_and(q < Z, below >= 0))
            yield above, jnp.logical_and(q >= max(low, 1), above < Z)

        def one_round(r, carry):
            for way, (zz, ok) in enumerate(places(r, 1)):
                @pl.when(ok)
                def _():
                    for part in (0, 2):
                        z_copy(way, zz, part).wait_recv()

                        @pl.when(z < Z - 1 if way == 0 else z > 0)
                        def _():
                            z_copy(way, zz, part).start()

                        x_copy(x, zz, part).start()
                        if part == 0:
                            y_copy(x, zz, 0).start()
                        c_copy(x, c, zz, part).start()

            for zz, ok in places(r - 1, 0):
                @pl.when(ok)
                def _():
                    for part in (0, 2):
                        x_copy(1 - x, zz, part).wait_recv()
                        if part == 0:
                            y_copy(1 - x, zz, 0).start()
                        c_copy(1 - x, c, zz, part).start()

            @pl.when(z == r)
            def _():
                pass_state()

            for zz, ok in places(r - 1, 1):
                @pl.when(ok)
                def _():
                    y_copy(x, zz, 1).wait_recv()
                    c_copy(x, c, zz, 1).start()
                    multiply(shard(x, c, zz), wbuf[shard(x, c, zz)])

            for zz, ok in places(r - 2, 0):
                @pl.when(ok)
                def _():
                    y_copy(1 - x, zz, 1).wait_recv()
                    c_copy(1 - x, c, zz, 1).start()
                    multiply(shard(1 - x, c, zz), wbuf[shard(1 - x, c, zz)])

                @pl.when(ok)
                def _():
                    for part in (0, 1, 2):
                        c_copy(x, 1 - c, zz, part).wait_recv()
                    multiply(shard(x, 1 - c, zz), wbuf[shard(x, 1 - c, zz)])

            for zz, ok in places(r - 3, 0):
                @pl.when(ok)
                def _():
                    for part in (0, 1, 2):
                        c_copy(1 - x, 1 - c, zz, part).wait_recv()
                    multiply(shard(1 - x, 1 - c, zz), wbuf[shard(1 - x, 1 - c, zz)])

            return carry

        lax.fori_loop(1, Z + 3, one_round, 0)
    else:
        acc[...] = jnp.zeros_like(acc)

        def one_block(at, carry):
            multiply(at, wown[pl.ds(pl.multiple_of(at * rows, 16), rows), :])
            return carry

        lax.fori_loop(0, features // rows, one_block, 0)

    info = info_in[...]
    for h in range(heads):
        q = acc[:, h * dk:(h + 1) * dk].astype(jnp.bfloat16)
        values = vv[:, h * dv:(h + 1) * dv]
        scores = dot(q, kv[:, h * dk:(h + 1) * dk], ((1,), (1,)))
        weighted = (scores * prob[h]).astype(jnp.bfloat16)
        inner = dot(weighted, values)
        inner_den = jnp.sum(weighted.astype(jnp.float32), axis=1, keepdims=True)
        cross = dot(q, mem_in[h])
        normer = info[h:h + 1, :].astype(jnp.bfloat16).astype(jnp.float32)
        cross_den = jnp.sum(q.astype(jnp.float32) * normer, axis=1, keepdims=True)
        top = imax_scr[:, h:h + 1]
        carried = jnp.where(count_col == 0, cum_col(h) + info[heads + h:heads + h + 1, 0:1], very_low)
        row_max = jnp.maximum(top, carried)
        a = jnp.exp(top - row_max)
        b = jnp.exp(carried - row_max) * factor
        den = a * inner_den + b * cross_den
        inverse = 1.0 / jnp.maximum(jnp.abs(den), jnp.exp(jnp.maximum(-row_max, 0.0)))
        hidden = (a * inverse) * inner + (b * inverse) * cross
        out_ref[0, :, h * dv:(h + 1) * dv] = hidden.astype(jnp.bfloat16)

    @pl.when(z < Z - 1)
    def _():
        info_copy().wait_send()
        for h in range(heads):
            mem_copy(h).wait_send()

    if spread:
        def drain(zz, carry):
            for part in (0, 2):
                @pl.when(jnp.logical_and(z < Z - 1, zz <= z))
                def _():
                    z_copy(0, zz, part).wait_send()

                @pl.when(jnp.logical_and(z > 0, zz >= z))
                def _():
                    z_copy(1, zz, part).wait_send()

                x_copy(x, zz, part).wait_send()

            @pl.when(zz != z)
            def _():
                y_copy(x, zz, 0).wait_send()

            y_copy(1 - x, zz, 0).wait_send()
            for xx in (x, 1 - x):
                for part in (0, 1, 2):
                    c_copy(xx, c, zz, part).wait_send()
            return carry

        lax.fori_loop(0, Z, drain, 0)


def body(Z, dp, planes, normed_input, query_weight, key_vectors, value_vectors, input_gate, forget_gate, resets):
    _, length, features = normed_input.shape
    heads = input_gate.shape[1]
    width = query_weight.shape[1]
    dk = key_vectors.shape[2] // heads
    dv = value_vectors.shape[2] // heads
    spread = dp == 4 and planes == 2 and query_weight.shape[0] % 128 == 0
    if spread:
        rows = query_weight.shape[0]
        weight = query_weight
    else:
        rows = 256
        weight = lax.all_gather(query_weight, ("dp", "ctx"), axis=0, tiled=True)
    count = features // rows if spread else 1
    dma = pltpu.SemaphoreType.DMA
    any_spec = pl.BlockSpec(memory_space=pl.ANY)
    vmem = pl.BlockSpec(memory_space=pltpu.VMEM)
    return pl.pallas_call(
        functools.partial(kernel, spread, Z, heads),
        out_shape=jax.ShapeDtypeStruct((1, length, heads * dv), jnp.bfloat16),
        in_specs=[any_spec] * 4 + [vmem] * 3,
        out_specs=vmem,
        scratch_shapes=[
            pltpu.VMEM((length, features), jnp.bfloat16),
            pltpu.VMEM((length, heads * dk), jnp.bfloat16),
            pltpu.VMEM((length, heads * dv), jnp.bfloat16),
            pltpu.VMEM(weight.shape, jnp.bfloat16),
            pltpu.VMEM((count, rows, width), jnp.bfloat16),
            pltpu.VMEM((length, width), jnp.float32),
            pltpu.VMEM((heads, length, length), jnp.float32),
            pltpu.VMEM((128, length), jnp.float32),
            pltpu.VMEM((length, 128), jnp.float32),
            pltpu.VMEM((heads, dk, dv), jnp.float32),
            pltpu.VMEM((2 * heads, dk), jnp.float32),
            pltpu.VMEM((heads, dk, dv), jnp.bfloat16),
            pltpu.VMEM((2 * heads, dk), jnp.float32),
            pltpu.VMEM((heads, dk, dv), jnp.bfloat16),
            pltpu.VMEM((2 * heads, dk), jnp.float32),
            dma((4,)),
            dma((2, Z, 2)), dma((Z, 2)),
            dma((Z, 2)), dma((Z, 2)),
            dma((2, Z)), dma((2, Z)),
            dma((2, Z, 3)), dma((2, Z, 3)),
            dma((heads + 1,)), dma((heads + 1,)),
        ],
        compiler_params=pltpu.CompilerParams(
            collective_id=0, has_side_effects=True, vmem_limit_bytes=40 * 1024 * 1024
        ),
        cost_estimate=pl.CostEstimate(
            flops=2 * length * features * width, bytes_accessed=6 * 1024 * 1024, transcendentals=0
        ),
    )(normed_input, weight, key_vectors, value_vectors, input_gate, forget_gate, resets)


def solution(mesh):
    sizes = mesh.shape
    return jax.shard_map(
        functools.partial(body, sizes["ctx"], sizes["dp"], sizes["groups"]),
        mesh=mesh,
        in_specs=(
            P(("groups", "dp"), "ctx", None),
            P(("dp", "ctx"), None),
            P(("groups", "dp"), "ctx", None),
            P(("groups", "dp"), "ctx", None),
            P(("groups", "dp"), None, "ctx"),
            P(("groups", "dp"), None, "ctx"),
            P(("groups", "dp"), "ctx"),
        ),
        out_specs=P(("groups", "dp"), "ctx", None),
        check_vma=False,
    )
```

time: 204 us -> 56.5 us (0.28)
  the two profiles are of different devices: /device:TPU:0 before, /device:TPU:24 now
where the time goes in v1:
time: 56.5 us; the launch traced here: 55.4 us
  Pallas kernels  47.9 us (85%)
  local copies, waits for them, and re-layouts  7.56 us (13%)
    pallas_call x1, Pallas kernels, body(): pl.pallas_call(functools.partial(kernel, spread, Z, heads), out_shape=jax...  47.9 us
    unnamed x15, local copies, waits for them, and re-layouts  7.56 us

profile of v1, /device:TPU:24, one launch (start us, length us, event | category | flops | bytes accessed | tf_op | source)
XLA Modules:
  0.0 55.4 jit_solution(16701249808390844701)
XLA Ops:
  0.0 0.0 copy-start
  0.0 1.6 %copy-done = bf16[1,256,4096]{2,1,0:T(8,128)(2,1)S(1)} copy-done((bf16[1,256,4096]{2,1,0:T(8,128)(2,1)S(1)}, bf16[1,256,4096]{2,1,0:T(8,128)(2,1)}, u32[]{:S(2)}) %copy-start) | copy-done | bytes 2097176
  1.6 0.0 copy-start.1
  1.6 1.0 %copy-done.1 = bf16[256,1024]{1,0:T(8,128)(2,1)S(1)} copy-done((bf16[256,1024]{1,0:T(8,128)(2,1)S(1)}, bf16[256,1024]{1,0:T(8,128)(2,1)}, u32[]{:S(2)}) %copy-start.1) | copy-done | bytes 524312
  2.6 0.0 copy-start.2
  2.6 1.0 %copy-done.2 = bf16[1,256,1024]{2,1,0:T(8,128)(2,1)S(1)} copy-done((bf16[1,256,1024]{2,1,0:T(8,128)(2,1)S(1)}, bf16[1,256,1024]{2,1,0:T(8,128)(2,1)}, u32[]{:S(2)}) %copy-start.2) | copy-done | bytes 524312
  3.7 0.0 copy-start.3
  3.7 1.0 %copy-done.3 = bf16[1,256,1024]{2,1,0:T(8,128)(2,1)S(1)} copy-done((bf16[1,256,1024]{2,1,0:T(8,128)(2,1)S(1)}, bf16[1,256,1024]{2,1,0:T(8,128)(2,1)}, u32[]{:S(2)}) %copy-start.3) | copy-done | bytes 524312
  4.7 0.0 copy-start.4
  4.7 0.7 %copy-done.4 = f32[1,4,256]{2,1,0:T(4,128)S(1)} copy-done((f32[1,4,256]{2,1,0:T(4,128)S(1)}, f32[1,4,256]{2,1,0:T(4,128)}, u32[]{:S(2)}) %copy-start.4) | copy-done | bytes 4120
  5.4 0.0 copy-start.5
  5.4 0.7 %copy-done.5 = f32[1,4,256]{2,1,0:T(4,128)S(1)} copy-done((f32[1,4,256]{2,1,0:T(4,128)S(1)}, f32[1,4,256]{2,1,0:T(4,128)}, u32[]{:S(2)}) %copy-start.5) | copy-done | bytes 4120
  6.1 0.0 copy-start.6
  6.1 0.7 %copy-done.6 = s32[1,256]{1,0:T(1,128)S(1)} copy-done((s32[1,256]{1,0:T(1,128)S(1)}, s32[1,256]{1,0:T(1,128)}, u32[]{:S(2)}) %copy-start.6) | copy-done | bytes 1048
  6.8 47.9 %shard_map.73 = bf16[1,256,1024]{2,1,0:T(8,128)(2,1)S(1)} custom-call(bf16[1,256,4096]{2,1,0:T(8,128)(2,1)S(1)} %copy-done, bf16[256,1024]{1,0:T(8,128)(2,1)S(1)} %copy-done.1, bf16[1,256,1024]{2,1,0:T(8,128)(2,1)S(1)} %copy-done.2, bf16[1,256,1024]{2,1,0:T(8,128)(2,1)S(1)} %copy-done.3, f32[1,4,256]{2,1,0:T(4,128)S(1)} %copy-done.4, ...), custom_call_target="tpu_custom_call" | custom-call | flops 2147483648 | bytes 6291456 | tf_op jit(solution)/shard_map/pallas_call | solution.py:380
  54.7 0.8 %copy.9 = bf16[1,256,1024]{2,1,0:T(8,128)(2,1)} copy(bf16[1,256,1024]{2,1,0:T(8,128)(2,1)S(1)} %shard_map.73) | data formatting | bytes 1048576
Async XLA Ops:
  0.0 1.6 %copy-start = (bf16[1,256,4096]{2,1,0:T(8,128)(2,1)S(1)}, bf16[1,256,4096]{2,1,0:T(8,128)(2,1)}, u32[]{:S(2)}) copy-start(bf16[1,256,4096]{2,1,0:T(8,128)(2,1)} %x_hbm.1) | copy-start | bytes 6291460
  1.6 1.0 %copy-start.1 = (bf16[256,1024]{1,0:T(8,128)(2,1)S(1)}, bf16[256,1024]{1,0:T(8,128)(2,1)}, u32[]{:S(2)}) copy-start(bf16[256,1024]{1,0:T(8,128)(2,1)} %w_hbm.1) | copy-start | bytes 1572868
  2.6 1.0 %copy-start.2 = (bf16[1,256,1024]{2,1,0:T(8,128)(2,1)S(1)}, bf16[1,256,1024]{2,1,0:T(8,128)(2,1)}, u32[]{:S(2)}) copy-start(bf16[1,256,1024]{2,1,0:T(8,128)(2,1)} %k_hbm.1) | copy-start | bytes 1572868
  3.7 1.0 %copy-start.3 = (bf16[1,256,1024]{2,1,0:T(8,128)(2,1)S(1)}, bf16[1,256,1024]{2,1,0:T(8,128)(2,1)}, u32[]{:S(2)}) copy-start(bf16[1,256,1024]{2,1,0:T(8,128)(2,1)} %v_hbm.1) | copy-start | bytes 1572868
  4.7 0.7 %copy-start.4 = (f32[1,4,256]{2,1,0:T(4,128)S(1)}, f32[1,4,256]{2,1,0:T(4,128)}, u32[]{:S(2)}) copy-start(f32[1,4,256]{2,1,0:T(4,128)} %ig_ref.1) | copy-start | bytes 12292
  5.4 0.7 %copy-start.5 = (f32[1,4,256]{2,1,0:T(4,128)S(1)}, f32[1,4,256]{2,1,0:T(4,128)}, u32[]{:S(2)}) copy-start(f32[1,4,256]{2,1,0:T(4,128)} %fg_ref.1) | copy-start | bytes 12292
  6.1 0.7 %copy-start.6 = (s32[1,256]{1,0:T(1,128)S(1)}, s32[1,256]{1,0:T(1,128)}, u32[]{:S(2)}) copy-start(s32[1,256]{1,0:T(1,128)} %rs_ref.1) | copy-start | bytes 3076
